TPU v7x, 32 devices: a whole 2x2x4 slice. The times are simulated.
32 devices in a mesh: expert: 4 (over x, core), context: 2 (over y), dp: 4 (over z).
Axes of the slice: x: 2, y: 2, z: 4, core: 2. Of those that a mesh axis runs over, the one named last changes fastest.
Arguments:
- tokens: bfloat16 [16, 512, 1024], P(('expert', 'dp'), 'context'), may hold values from -6 to 6
- span_order: int32 [4], replicated, may hold values from 0 to 3, each once
- routes: int32 [16, 512, 8], P(('expert', 'dp'), 'context'), may hold values from 0 to 15, all different within a row; in each aligned block of 256 rows (0 to 255, 256 to 511, ..., all dimensions but the last counted through in order) at most 160 rows name the same one
- norm_attn: bfloat16 [1024], replicated, may hold values from 0.5 to 1.5
- w_query: bfloat16 [1024, 1024], replicated, may hold values from -0.1875 to 0.1875
- w_key: bfloat16 [1024, 512], replicated, may hold values from -0.1875 to 0.1875
- w_value: bfloat16 [1024, 512], replicated, may hold values from -0.1875 to 0.1875
- w_out: bfloat16 [1024, 1024], replicated, may hold values from -1.5 to 1.5
- norm_moe: bfloat16 [1024], replicated, may hold values from 0.5 to 1.5
- w_router: bfloat16 [1024, 16], replicated, may hold values from -0.09375 to 0.09375
- w_gate: bfloat16 [16, 1024, 512], P('expert'), may hold values from -0.1875 to 0.1875
- w_up: bfloat16 [16, 1024, 512], P('expert'), may hold values from -0.1875 to 0.1875
- w_down: bfloat16 [16, 512, 1024], P('expert'), may hold values from -1 to 1
- cotangent: bfloat16 [16, 512, 1024], P(('expert', 'dp'), 'context'), may hold values from -6 to 6
Outputs:
- outputs: bfloat16 [16, 512, 1024], P(('expert', 'dp'), 'context')
- grad_tokens: bfloat16 [16, 512, 1024], P(('expert', 'dp'), 'context')
- grad_norm_attn: float32 [1024], replicated
- grad_query: float32 [1024, 1024], replicated
- grad_key: float32 [1024, 512], replicated
- grad_value: float32 [1024, 512], replicated
- grad_out: float32 [1024, 1024], replicated
- grad_norm_moe: float32 [1024], replicated
- grad_router: float32 [1024, 16], replicated
- grad_gate: float32 [16, 1024, 512], P('expert')
- grad_up: float32 [16, 1024, 512], P('expert')
- grad_down: float32 [16, 512, 1024], P('expert')
Inputs may be any that keep to these rules, and one draw needn't show every extreme that they name: span_order is a permutation; stored block j of every sequence holds the tokens at positions span_order[j] * 128 to span_order[j] * 128 + 127. `routes`: each token names 8 different experts. Within the rows of one device (aligned blocks of 256 rows, in order), no expert is named by more than 160 rows, a bound that some block reaches.
All inputs are finite; a program needn't handle non-finite values.
Results may differ from a plain program's by a relative error of at most 0.017.
Values may be sent and summed in bfloat16 or wider, within the bound.
A program may use at most 192 MiB of HBM per device.

v0:
```python
import math
import jax
import jax.numpy as jnp
from jax import lax
from jax.sharding import PartitionSpec as P

D = 1024
H = 16
KV = 8
HD = 64
TOP = 8
EXPERTS = 16
CAP = 160
SPAN = 128
EPSILON = 1e-06
ROPE_BASE = 10000.0
MASKED = -1e30


def rope_tables(positions):
    half_dim = HD // 2
    frequency = ROPE_BASE ** (-(jnp.arange(half_dim, dtype=jnp.float32) * 2.0) / HD)
    angles = positions.astype(jnp.float32)[:, None] * frequency[None, :]
    return (jnp.cos(angles), jnp.sin(angles))


def rotate(tensor, cos_table, sin_table):
    half_dim = tensor.shape[-1] // 2
    front_half = tensor[..., :half_dim]
    back_half = tensor[..., half_dim:]
    cos_wide = cos_table[:, None, :]
    sin_wide = sin_table[:, None, :]
    return jnp.concatenate(
        [
            front_half * cos_wide - back_half * sin_wide,
            back_half * cos_wide + front_half * sin_wide,
        ],
        axis=-1,
    )


def rotate_back(tensor, cos_table, sin_table):
    half_dim = tensor.shape[-1] // 2
    front_grad = tensor[..., :half_dim]
    back_grad = tensor[..., half_dim:]
    cos_wide = cos_table[:, None, :]
    sin_wide = sin_table[:, None, :]
    return jnp.concatenate(
        [
            front_grad * cos_wide + back_grad * sin_wide,
            back_grad * cos_wide - front_grad * sin_wide,
        ],
        axis=-1,
    )


def slot_tables(route_rows):
    flat_ids = route_rows.reshape(-1)
    assignments = flat_ids.shape[0]
    one_hot = (flat_ids[:, None] == jnp.arange(EXPERTS, dtype=jnp.int32)[None, :]).astype(jnp.int32)
    earlier = jnp.cumsum(one_hot, axis=0, dtype=jnp.int32) - one_hot
    within = jnp.sum(earlier * one_hot, axis=1, dtype=jnp.int32)
    target = flat_ids * CAP + within
    source = (
        jnp.full((EXPERTS * CAP,), assignments, jnp.int32)
        .at[target]
        .set(jnp.arange(assignments, dtype=jnp.int32))
    )
    filled = source < assignments
    return (target, jnp.minimum(source, assignments - 1), filled)


def positions_of(row_index, span_order):
    block_ids = row_index // SPAN
    picked = jnp.where(
        block_ids[:, None] == jnp.arange(span_order.shape[0], dtype=jnp.int32)[None, :],
        span_order[None, :],
        0,
    )
    return jnp.sum(picked, axis=1, dtype=jnp.int32) * SPAN + row_index % SPAN


def norm_back(grad_normed, normed, inv_root):
    return inv_root * (
        grad_normed - normed * jnp.mean(grad_normed * normed, axis=-1, keepdims=True)
    )


def body(
    tokens,
    span_order,
    routes,
    norm_attn,
    w_query,
    w_key,
    w_value,
    w_out,
    norm_moe,
    w_router,
    w_gate,
    w_up,
    w_down,
    cotangent,
):
    tok_rows = tokens.shape[1]
    seq_rows = tok_rows * lax.axis_size("context")
    groups = H // KV
    score_scale = 1.0 / math.sqrt(HD)
    local_experts = w_gate.shape[0]
    expert_groups = lax.axis_size("expert")
    local_index = lax.axis_index("context") * tok_rows + jnp.arange(tok_rows, dtype=jnp.int32)
    pos_query = positions_of(local_index, span_order)
    pos_keys = positions_of(jnp.arange(seq_rows, dtype=jnp.int32), span_order)
    cos_table, sin_table = rope_tables(pos_query)
    allowed = pos_keys[None, :] <= pos_query[:, None]
    inputs = tokens[0].astype(jnp.float32)
    inv_one = lax.rsqrt(jnp.mean(inputs * inputs, axis=-1, keepdims=True) + EPSILON)
    normed_one = inputs * inv_one
    gain_one = norm_attn.astype(jnp.float32)
    h_one = (normed_one * gain_one).astype(jnp.bfloat16)
    query_pre = jnp.dot(h_one, w_query, preferred_element_type=jnp.float32).reshape(tok_rows, H, HD)
    queries = (
        rotate(query_pre, cos_table, sin_table)
        .astype(jnp.bfloat16)
        .reshape(tok_rows, KV, groups, HD)
    )
    key_pre = jnp.dot(h_one, w_key, preferred_element_type=jnp.float32).reshape(tok_rows, KV, HD)
    keys_local = (
        rotate(key_pre, cos_table, sin_table).astype(jnp.bfloat16).reshape(tok_rows, KV * HD)
    )
    values_local = jnp.dot(h_one, w_value, preferred_element_type=jnp.float32).astype(jnp.bfloat16)
    keys_all, values_all = (
        lax.all_gather(keys_local, "context", axis=0, tiled=True),
        lax.all_gather(values_local, "context", axis=0, tiled=True),
    )
    scores = (
        jnp.einsum(
            "qkgd,skd->kgqs",
            queries,
            keys_all.reshape(seq_rows, KV, HD),
            preferred_element_type=jnp.float32,
        )
        * score_scale
    )
    masked = jnp.where(allowed, scores, MASKED)
    top_score = jnp.max(masked, axis=-1, keepdims=True)
    exp_scores = jnp.exp(masked - top_score)
    total_exp = jnp.sum(exp_scores, axis=-1, keepdims=True)
    attn_probs = exp_scores / total_exp
    log_total = top_score + jnp.log(total_exp)
    mixed_heads = jnp.einsum(
        "kgqs,skd->qkgd",
        attn_probs.astype(jnp.bfloat16),
        values_all.reshape(seq_rows, KV, HD),
        preferred_element_type=jnp.float32,
    )
    mixed_heads = mixed_heads.reshape(tok_rows, H * HD).astype(jnp.bfloat16)
    y_one = inputs + jnp.dot(mixed_heads, w_out, preferred_element_type=jnp.float32)
    inv_two = lax.rsqrt(jnp.mean(y_one * y_one, axis=-1, keepdims=True) + EPSILON)
    normed_two = y_one * inv_two
    gain_two = norm_moe.astype(jnp.float32)
    h_two = (normed_two * gain_two).astype(jnp.bfloat16)
    logits = jnp.dot(h_two, w_router, preferred_element_type=jnp.float32)
    route_rows = routes[0]
    chosen_mask = route_rows[:, :, None] == jnp.arange(EXPERTS, dtype=jnp.int32)[None, None, :]
    chosen = jnp.sum(jnp.where(chosen_mask, logits[:, None, :], 0.0), axis=-1)
    chosen_exp = jnp.exp(chosen - jnp.max(chosen, axis=-1, keepdims=True))
    route_weights = chosen_exp / jnp.sum(chosen_exp, axis=-1, keepdims=True)
    target, source, filled = slot_tables(route_rows)
    sent_rows = jnp.where(
        filled[:, None], jnp.take(h_two, source // TOP, axis=0), jnp.zeros((), jnp.bfloat16)
    )
    sent_rows = sent_rows.reshape(expert_groups, local_experts, CAP, D)
    received = lax.all_to_all(sent_rows, "expert", split_axis=0, concat_axis=0, tiled=True)
    gate_pre = jnp.einsum("necd,edf->necf", received, w_gate, preferred_element_type=jnp.float32)
    upward = jnp.einsum("necd,edf->necf", received, w_up, preferred_element_type=jnp.float32)
    sigmoid_gate = jax.nn.sigmoid(gate_pre)
    silu_gate = gate_pre * sigmoid_gate
    hidden = (silu_gate * upward).astype(jnp.bfloat16)
    produced = jnp.einsum(
        "necf,efd->necd", hidden, w_down, preferred_element_type=jnp.float32
    ).astype(jnp.bfloat16)
    returned = lax.all_to_all(produced, "expert", split_axis=0, concat_axis=0, tiled=True).reshape(
        EXPERTS * CAP, D
    )
    gathered = jnp.take(returned, target, axis=0).reshape(tok_rows, TOP, D).astype(jnp.float32)
    y_two = jnp.sum(route_weights[:, :, None] * gathered, axis=1)
    outputs = (y_one + y_two).astype(jnp.bfloat16)[None]
    grad_final = cotangent[0].astype(jnp.float32)
    grad_gathered = route_weights[:, :, None] * grad_final[:, None, :]
    grad_weights = jnp.sum(grad_final[:, None, :] * gathered, axis=-1)
    grad_slots = jnp.where(
        filled[:, None], jnp.take(grad_gathered.reshape(-1, D), source, axis=0), 0.0
    )
    grad_slots = grad_slots.astype(jnp.bfloat16).reshape(expert_groups, local_experts, CAP, D)
    grad_received = lax.all_to_all(grad_slots, "expert", split_axis=0, concat_axis=0, tiled=True)
    grad_hidden = jnp.einsum(
        "necd,efd->necf", grad_received, w_down, preferred_element_type=jnp.float32
    )
    grad_down_w = jnp.einsum(
        "necf,necd->efd", hidden, grad_received, preferred_element_type=jnp.float32
    )
    grad_gate_pre = (
        grad_hidden * upward * sigmoid_gate * (1.0 + gate_pre * (1.0 - sigmoid_gate))
    ).astype(jnp.bfloat16)
    grad_up_pre = (grad_hidden * silu_gate).astype(jnp.bfloat16)
    grad_gate_w = jnp.einsum(
        "necd,necf->edf", received, grad_gate_pre, preferred_element_type=jnp.float32
    )
    grad_up_w = jnp.einsum(
        "necd,necf->edf", received, grad_up_pre, preferred_element_type=jnp.float32
    )
    grad_sent = jnp.einsum(
        "necf,edf->necd", grad_gate_pre, w_gate, preferred_element_type=jnp.float32
    )
    grad_sent = (
        grad_sent
        + jnp.einsum("necf,edf->necd", grad_up_pre, w_up, preferred_element_type=jnp.float32)
    ).astype(jnp.bfloat16)
    grad_back = lax.all_to_all(
        grad_sent, "expert", split_axis=0, concat_axis=0, tiled=True
    ).reshape(EXPERTS * CAP, D)
    grad_h_two = jnp.sum(
        jnp.take(grad_back, target, axis=0).reshape(tok_rows, TOP, D).astype(jnp.float32), axis=1
    )
    grad_chosen = route_weights * (
        grad_weights - jnp.sum(route_weights * grad_weights, axis=-1, keepdims=True)
    )
    grad_logits = jnp.sum(jnp.where(chosen_mask, grad_chosen[:, :, None], 0.0), axis=1).astype(
        jnp.bfloat16
    )
    grad_router_w = jnp.einsum("td,te->de", h_two, grad_logits, preferred_element_type=jnp.float32)
    grad_h_two = grad_h_two + jnp.einsum(
        "te,de->td", grad_logits, w_router, preferred_element_type=jnp.float32
    )
    grad_gain_two = jnp.sum(grad_h_two * normed_two, axis=0)
    grad_y_one = grad_final + norm_back(grad_h_two * gain_two, normed_two, inv_two)
    grad_attn = grad_y_one.astype(jnp.bfloat16)
    grad_out_w = jnp.einsum("tm,td->md", mixed_heads, grad_attn, preferred_element_type=jnp.float32)
    grad_mixed = jnp.einsum(
        "td,md->tm", grad_attn, w_out, preferred_element_type=jnp.float32
    ).astype(jnp.bfloat16)
    grad_mixed = grad_mixed.reshape(tok_rows, KV, groups, HD)
    keys_back, values_back = (
        lax.all_gather(keys_local, "context", axis=0, tiled=True),
        lax.all_gather(values_local, "context", axis=0, tiled=True),
    )
    key_heads = keys_back.reshape(seq_rows, KV, HD)
    scores_back = (
        jnp.einsum("qkgd,skd->kgqs", queries, key_heads, preferred_element_type=jnp.float32)
        * score_scale
    )
    probs_back = jnp.where(allowed, jnp.exp(scores_back - log_total), 0.0)
    grad_probs = jnp.einsum(
        "qkgd,skd->kgqs",
        grad_mixed,
        values_back.reshape(seq_rows, KV, HD),
        preferred_element_type=jnp.float32,
    )
    grad_values = jnp.einsum(
        "kgqs,qkgd->skd",
        probs_back.astype(jnp.bfloat16),
        grad_mixed,
        preferred_element_type=jnp.float32,
    )
    row_dots = jnp.sum(probs_back * grad_probs, axis=-1, keepdims=True)
    grad_scores = (probs_back * (grad_probs - row_dots)).astype(jnp.bfloat16)
    grad_queries = (
        jnp.einsum("kgqs,skd->qkgd", grad_scores, key_heads, preferred_element_type=jnp.float32)
        * score_scale
    )
    grad_keys = (
        jnp.einsum("kgqs,qkgd->skd", grad_scores, queries, preferred_element_type=jnp.float32)
        * score_scale
    )
    grad_keys_mine, grad_values_mine = (
        lax.psum_scatter(
            grad_keys.reshape(seq_rows, KV * HD), "context", scatter_dimension=0, tiled=True
        ),
        lax.psum_scatter(
            grad_values.reshape(seq_rows, KV * HD), "context", scatter_dimension=0, tiled=True
        ),
    )
    grad_q_pre = (
        rotate_back(grad_queries.reshape(tok_rows, H, HD), cos_table, sin_table)
        .reshape(tok_rows, H * HD)
        .astype(jnp.bfloat16)
    )
    grad_k_pre = (
        rotate_back(grad_keys_mine.reshape(tok_rows, KV, HD), cos_table, sin_table)
        .reshape(tok_rows, KV * HD)
        .astype(jnp.bfloat16)
    )
    grad_v_pre = grad_values_mine.astype(jnp.bfloat16)
    grad_query_w = jnp.einsum("td,tm->dm", h_one, grad_q_pre, preferred_element_type=jnp.float32)
    grad_key_w = jnp.einsum("td,tm->dm", h_one, grad_k_pre, preferred_element_type=jnp.float32)
    grad_value_w = jnp.einsum("td,tm->dm", h_one, grad_v_pre, preferred_element_type=jnp.float32)
    grad_h_one = jnp.einsum("tm,dm->td", grad_q_pre, w_query, preferred_element_type=jnp.float32)
    grad_h_one = grad_h_one + jnp.einsum(
        "tm,dm->td", grad_k_pre, w_key, preferred_element_type=jnp.float32
    )
    grad_h_one = grad_h_one + jnp.einsum(
        "tm,dm->td", grad_v_pre, w_value, preferred_element_type=jnp.float32
    )
    grad_gain_one = jnp.sum(grad_h_one * normed_one, axis=0)
    grad_inputs = grad_y_one + norm_back(grad_h_one * gain_one, normed_one, inv_one)
    grad_tokens = grad_inputs.astype(jnp.bfloat16)[None]
    total_gate, total_up, total_down = (
        lax.psum(grad_gate_w.astype(jnp.bfloat16), ("context", "dp")).astype(jnp.float32),
        lax.psum(grad_up_w.astype(jnp.bfloat16), ("context", "dp")).astype(jnp.float32),
        lax.psum(grad_down_w.astype(jnp.bfloat16), ("context", "dp")).astype(jnp.float32),
    )
    total_g1, total_q, total_k, total_v, total_o, total_g2, total_r = lax.psum(
        (
            grad_gain_one,
            grad_query_w,
            grad_key_w,
            grad_value_w,
            grad_out_w,
            grad_gain_two,
            grad_router_w,
        ),
        ("expert", "context", "dp"),
    )
    return (
        outputs,
        grad_tokens,
        total_g1,
        total_q,
        total_k,
        total_v,
        total_o,
        total_g2,
        total_r,
        total_gate,
        total_up,
        total_down,
    )


def solution(mesh):
    in_specs = (
        P(("expert", "dp"), "context", None),
        P(),
        P(("expert", "dp"), "context", None),
        P(),
        P(),
        P(),
        P(),
        P(),
        P(),
        P(),
        P("expert", None, None),
        P("expert", None, None),
        P("expert", None, None),
        P(("expert", "dp"), "context", None),
    )
    out_specs = (
        P(("expert", "dp"), "context", None),
        P(("expert", "dp"), "context", None),
        P(),
        P(),
        P(),
        P(),
        P(),
        P(),
        P(),
        P("expert", None, None),
        P("expert", None, None),
        P("expert", None, None),
    )
    return jax.shard_map(body, mesh=mesh, in_specs=in_specs, out_specs=out_specs, check_vma=False)
```

profile of v0, /device:TPU:0, one launch (start us, length us, event | category | flops | bytes accessed | tf_op | source)
XLA Modules:
  0.0 1157.8 jit_solution(6361689802056740667)
XLA Ops:
  13.8 9.9 all_gather.8
  30.6 8.2 all_gather.9
  38.8 4.1 copy.81
  42.9 2.4 fusion.70
  53.3 4.5 reduce-window.6
  58.7 8.1 scatter_custom_fusion
  68.4 8.8 gather_fusion
  77.2 3.7 select_select_fusion
  80.9 62.5 %all_to_all.20 = bf16[4,4,160,1024]{3,2,1,0:T(8,128)(2,1)S(1)} all-to-all(bf16[4,4,160,1024]{3,2,1,0:T(8,128)(2,1)S(1)} %select_select_fusion), channel_id=1, replica_groups=mesh['expert'=4,'context'=2,'dp'=4] {'expert'}, dimensions={0} | all-to-all | bytes 10485760 | tf_op jit(solution)/shard_map/all_to_all | solution.py:174
  143.4 2.9 fusion.26
  147.4 5.4 fusion.15
  153.1 4.9 convert_bitcast_fusion.1
  157.9 3.3 copy.89
  161.2 5.2 all-to-all-start.1
  168.0 57.9 %all-to-all-done.1 = bf16[4,4,160,1024]{3,2,1,0:T(8,128)(2,1)} async-done(((bf16[4,4,160,1024]{3,2,1,0:T(8,128)(2,1)}), bf16[4,4,160,1024]{3,2,1,0:T(8,128)(2,1)}, u32[]{:S(2)}, u32[]{:S(2)}) %all-to-all-start.1) | async-done | bytes 5242912 | tf_op jit(solution)/shard_map/all_to_all | solution.py:183
  225.9 14.1 %gather_fusion.2 = bf16[2048,1024]{1,0:T(8,128)(2,1)} fusion(bf16[2560,1024]{1,0:T(8,128)(2,1)} %bitcast.33, s32[2048]{0:T(1024)S(1)} %broadcast_clamp_fusion), kind=kCustom, calls=%fused_computation.clone | custom fusion | bytes 8396800 | tf_op jit(solution)/shard_map/jit(_take)/gather | solution.py:186
  240.0 3.3 fusion.2
  243.7 3.4 bitcast_multiply_fusion.1
  247.1 14.8 %gather_fusion.1 = bf16[2560,1024]{1,0:T(8,128)(2,1)} fusion(bf16[2048,1024]{1,0:T(8,128)(2,1)} %bitcast_multiply_fusion.1, s32[3072]{0:T(1024)S(1)} %pad_clamp_fusion), kind=kCustom, calls=%fused_computation.3 | custom fusion | bytes 10496000 | tf_op jit(solution)/shard_map/jit(_take)/gather | solution.py:193
  261.9 4.0 select_convert_fusion
  265.9 63.3 %all_to_all.21 = bf16[4,4,160,1024]{3,2,1,0:T(8,128)(2,1)} all-to-all(bf16[4,4,160,1024]{3,2,1,0:T(8,128)(2,1)S(1)} %select_convert_fusion), channel_id=1, replica_groups=mesh['expert'=4,'context'=2,'dp'=4] {'expert'}, dimensions={0} | all-to-all | bytes 10485760 | tf_op jit(solution)/shard_map/all_to_all | solution.py:196
  329.2 12.7 %fusion.13 = (bf16[4,4,160,512]{3,2,0,1:T(8,128)(2,1)}, bf16[4,4,160,512]{3,2,0,1:T(8,128)(2,1)S(1)}) fusion(f32[4,4,160,512]{3,2,1,0:T(8,128)} %get-tuple-element.56, f32[4,4,160,512]{3,2,1,0:T(8,128)} %copy-done.45, bf16[4,512,1024]{2,1,0:T(8,128)(2,1)} %param.28, bf16[4,4,160,1024]{3,2,1,0:T(8,128)(2,1)} %all_to_all.21), kind=kOutput, calls=%fused_computation.35 | convolution fusion | flops 2701393920 | bytes 25165824 | tf_op jit(solution)/shard_map/necd,efd->necf/dot_general | solution.py:197
  342.0 8.6 fusion.29
  350.6 8.9 fusion.10
  359.5 3.0 copy.92
  362.5 5.1 all-to-all-start.3
  367.9 59.2 %all-to-all-done.3 = bf16[4,4,160,1024]{3,2,1,0:T(8,128)(2,1)} async-done(((bf16[4,4,160,1024]{3,2,1,0:T(8,128)(2,1)}), bf16[4,4,160,1024]{3,2,1,0:T(8,128)(2,1)}, u32[]{:S(2)}, u32[]{:S(2)}) %all-to-all-start.3) | async-done | bytes 5242912 | tf_op jit(solution)/shard_map/all_to_all | solution.py:220
  427.1 14.1 %gather_fusion.3 = bf16[2048,1024]{1,0:T(8,128)(2,1)} fusion(bf16[2560,1024]{1,0:T(8,128)(2,1)} %bitcast.45, s32[2048]{0:T(1024)S(1)} %broadcast_clamp_fusion), kind=kCustom, calls=%fused_computation.1.clone | custom fusion | bytes 8396800 | tf_op jit(solution)/shard_map/jit(_take)/gather | solution.py:224
  441.2 8.1 convert_reduce_fusion
  455.5 5.3 fusion.3
  461.6 2.4 fusion.5
  468.5 6.2 fusion.38
  475.0 8.9 bitcast_convert_fusion.2
  483.9 8.4 bitcast_convert_fusion.1
  492.4 5.1 bitcast_convert_fusion
  498.6 3.0 convolution_multiply_fusion
  502.0 3.1 fusion.76
  505.0 2.7 fusion.79
  512.6 2.9 fusion.82
  515.6 2.5 fusion.124
  521.6 42.8 %all-reduce = (f32[1024]{0:T(1024)}, f32[1024]{0:T(1024)}) all-reduce(f32[1024]{0:T(1024)S(1)} %get-tuple-element.15, f32[1024]{0:T(1024)S(1)} %get-tuple-element.13), channel_id=1, replica_groups=mesh['expert'=4,'context'=2,'dp'=4] {'expert','context','dp'}, use_global_device_ids=true, to_apply=%region_24.26 | all-reduce | flops 2048 | bytes 16384 | tf_op jit(solution)/shard_map/psum | solution.py:313
  564.3 2.6 fusion.69
  567.0 328.1 %all-reduce.8.cloned.1.call-done = (bf16[4,1024,512]{2,1,0:T(8,128)(2,1)}, bf16[4,1024,512]{2,1,0:T(8,128)(2,1)}, bf16[4,512,1024]{2,1,0:T(8,128)(2,1)}) async-done(((bf16[4,1024,512]{2,1,0:T(8,128)(2,1)}, bf16[4,1024,512]{2,1,0:T(8,128)(2,1)}, bf16[4,512,1024]{2,1,0:T(8,128)(2,1)}), (bf16[4,1024,512]{2,1,0:T(8,128)(2,1)}, bf16[4,1024,512]{2,1,0:T(8,128)(2,1)}, ...) | async-done | bytes 12582928 | tf_op jit(solution)/shard_map/psum | solution.py:309
  895.1 6.9 convert_element_type.232
  902.0 4.6 convert_element_type.234
  906.6 4.5 convert_element_type.236
  911.0 227.6 %all-reduce.6.cloned.1.call-done = (f32[1024,1024]{1,0:T(8,128)}, f32[1024,512]{1,0:T(8,128)}, f32[1024,512]{1,0:T(8,128)}, f32[1024,1024]{1,0:T(8,128)}, f32[1024,16]{0,1:T(8,128)}) async-done(((f32[1024,1024]{1,0:T(8,128)}, f32[1024,512]{1,0:T(8,128)}, f32[1024,512]{1,0:T(8,128)}, f32[1024,1024]{1,0:T(8,128)}, f32[1024,16]{0,1:T(8,128)}), (f32[1024,1024]{1,0:T(8,128)}, f32[1024,512]{1,0:T(8,128)}, ...) | async-done | bytes 12648464 | tf_op jit(solution)/shard_map/psum | solution.py:313
  1138.7 4.9 copy.142
  (194 shorter events, 54.3 us)
Async XLA Ops:
  8.0 43.3 %copy-start = (bf16[1024,1024]{1,0:T(8,128)(2,1)S(1)}, bf16[1024,1024]{1,0:T(8,128)(2,1)}, u32[]{:S(2)}) copy-start(bf16[1024,1024]{1,0:T(8,128)(2,1)} %param.23) | copy-start | bytes 6291460
  8.0 20.5 %copy-start.3 = (bf16[1,256,1024]{2,1,0:T(8,128)(2,1)S(1)}, bf16[1,256,1024]{2,1,0:T(8,128)(2,1)}, u32[]{:S(2)}) copy-start(bf16[1,256,1024]{2,1,0:T(8,128)(2,1)} %param.16) | copy-start | bytes 1572868
  10.7 32.2 %copy-start.36 = (f32[1024]{0:T(1024)}, f32[1024]{0:T(1024)S(1)}, u32[]{:S(2)}) copy-start(f32[1024]{0:T(1024)S(1)} %convert_element_type.188) | copy-start | bytes 12292
  11.9 31.0 %copy-start.41 = (f32[256]{0:T(256)}, f32[256]{0:T(256)S(1)}, u32[]{:S(2)}) copy-start(f32[256]{0:T(256)S(1)} %add_rsqrt_fusion.1) | copy-start | bytes 3076
  30.5 15.0 %copy-start.32 = (f32[256,32]{0,1:T(8,128)}, f32[256,32]{0,1:T(8,128)S(1)}, u32[]{:S(2)}) copy-start(f32[256,32]{0,1:T(8,128)S(1)} %get-tuple-element.49) | copy-start | bytes 98308
  30.5 15.0 %copy-start.34 = (f32[256,32]{0,1:T(8,128)}, f32[256,32]{0,1:T(8,128)S(1)}, u32[]{:S(2)}) copy-start(f32[256,32]{0,1:T(8,128)S(1)} %get-tuple-element.50) | copy-start | bytes 98308
  38.8 8.3 copy-start.8
  47.1 4.2 copy-start.1
  48.9 4.2 copy-start.43
  51.3 25.9 %copy-start.28 = (bf16[8,64,2,256]{3,1,2,0:T(8,128)(2,1)}, bf16[8,64,2,256]{3,1,2,0:T(8,128)(2,1)S(1)}, u32[]{:S(2)}) copy-start(bf16[8,64,2,256]{3,1,2,0:T(8,128)(2,1)S(1)} %fusion.57) | copy-start | bytes 1572868
  80.9 62.5 %copy-start.15 = (bf16[4,1024,512]{2,1,0:T(8,128)(2,1)S(1)}, bf16[4,1024,512]{2,1,0:T(8,128)(2,1)}, u32[]{:S(2)}) copy-start(bf16[4,1024,512]{2,1,0:T(8,128)(2,1)} %param.26) | copy-start | bytes 12582916
  143.4 4.1 copy-start.14
  147.4 5.6 copy-start.45
  147.4 5.6 copy-start.44
  161.2 5.3 copy-start.38
  161.2 5.5 copy-start.39
  161.2 5.7 copy-start.26
  161.2 64.7 %all-to-all-start.1 = ((bf16[4,4,160,1024]{3,2,1,0:T(8,128)(2,1)}), bf16[4,4,160,1024]{3,2,1,0:T(8,128)(2,1)}, u32[]{:S(2)}, u32[]{:S(2)}) async-start(bf16[4,4,160,1024]{3,2,1,0:T(8,128)(2,1)} %copy.89), calls=%async_computation.1 | async-start | bytes 10485760 | tf_op jit(solution)/shard_map/all_to_all | solution.py:183
  342.0 8.6 copy-start.16
  362.5 64.5 %all-to-all-start.3 = ((bf16[4,4,160,1024]{3,2,1,0:T(8,128)(2,1)}), bf16[4,4,160,1024]{3,2,1,0:T(8,128)(2,1)}, u32[]{:S(2)}, u32[]{:S(2)}) async-start(bf16[4,4,160,1024]{3,2,1,0:T(8,128)(2,1)} %copy.92), calls=%async_computation.3 | async-start | bytes 10485760 | tf_op jit(solution)/shard_map/all_to_all | solution.py:220
  367.6 140.2 %reduce-scatter.3.cloned.1.call-start = ((), (), s32[]{:S(2)}) async-start(), calls=%async_computation.6 | async-start | bytes 1572864 | tf_op jit(solution)/shard_map/reduce_scatter | solution.py:277
  441.2 8.1 copy-start.5
  441.2 8.6 copy-start.27
  449.8 5.8 copy-start.23
  455.5 5.3 slice-start
  455.5 6.1 slice-start.1
  461.6 4.4 copy-start.19
  461.6 4.4 copy-start.21
  468.4 44.2 %reduce-scatter.5.cloned.1.call-start = ((), (), s32[]{:S(2)}) async-start(), calls=%async_computation.7 | async-start | bytes 1572864 | tf_op jit(solution)/shard_map/reduce_scatter | solution.py:280
  474.7 420.3 %all-reduce.8.cloned.1.call-start = ((), (), s32[]{:S(2)}) async-start(), calls=%async_computation.9 | async-start | bytes 25165824 | tf_op jit(solution)/shard_map/psum | solution.py:309
  475.0 8.9 copy-start.17
  475.0 17.4 %slice-start.2 = ((s8[5242880]{0:T(1024)(128)(4,1)}), s8[4194304]{0:T(1024)(128)(4,1)S(1)}, s32[]{:S(2)}) async-start(s8[5242880]{0:T(1024)(128)(4,1)} %bitcast.293), calls=%async_computation.12 | async-start | bytes 8388608
  483.9 8.4 slice-start.3
  483.9 8.4 copy-start.46
  497.5 4.2 copy-start.33
  497.5 4.2 copy-start.35
  497.5 641.1 %all-reduce.6.cloned.1.call-start = ((), (), s32[]{:S(2)}) async-start(), calls=%async_computation.8 | async-start | bytes 25296896 | tf_op jit(solution)/shard_map/psum | solution.py:313
  498.6 3.3 copy-start.37
  498.6 3.3 copy-start.42
  501.7 3.4 copy-start.7
  501.7 3.4 copy-start.29
  515.6 4.2 copy-start.30
  515.6 4.2 copy-start.31
  895.1 6.9 copy-start.12
  902.0 4.6 copy-start.11
  1138.7 4.9 copy-start.25
  1138.7 6.3 copy-start.24
  1143.6 3.7 copy-start.13
  (9 other events, 17.3 us)
Sparse Core Ops, SparseCore 0:
  468.6 20.5 reduce-scatter.2
  492.1 20.4 reduce-scatter.4
Sparse Core Ops, SparseCore 1:
  497.6 397.4 all-reduce.7
  903.6 235.0 all-reduce.5
where the time goes:
time: 1170 us; the launch traced here: 1160 us
  waiting for transfers between devices  675 us (58%)
  blocking collectives  187 us (16%)
  matrix products  114 us (10%)
  local copies, waits for them, and re-layouts  94.5 us (8%)
  other arithmetic  60.2 us (5%)
  between operations  16.8 us (1%)
    psum x1, waiting for transfers between devices, body(): lax.psum(grad_gate_w.astype(jnp.bfloat16), ('context', 'dp'))  328 us
    psum x1, waiting for transfers between devices, body(): lax.psum((grad_gain_one, grad_query_w, grad_key_w, grad_value_w, grad_out...  228 us
    all_to_all x1, blocking collectives, body(): lax.all_to_all(grad_slots, 'expert', split_axis=0, concat_axis=0, tiled=T...  63.3 us
    all_to_all x1, blocking collectives, body(): lax.all_to_all(sent_rows, 'expert', split_axis=0, concat_axis=0, tiled=True)  62.5 us
    all_to_all x1, waiting for transfers between devices, body(): lax.all_to_all(grad_sent, 'expert', split_axis=0, concat_axis=0, tiled=True)  59.2 us
    all_to_all x1, waiting for transfers between devices, body(): lax.all_to_all(produced, 'expert', split_axis=0, concat_axis=0, tiled=True)  57.9 us
    psum x1, blocking collectives, body(): lax.psum((grad_gain_one, grad_query_w, grad_key_w, grad_value_w, grad_out...  42.8 us
    unnamed x110, local copies, waits for them, and re-layouts  23.9 us
  transfers between devices with their start and end apart: 6, of which 5 were waited for; matrix products, arithmetic and copies ran while one was open for 6% of the time, Pallas kernels for 0%

commit v1 on v0

--- a/solution.py
+++ b/solution.py
@@ -311,16 +311,19 @@
         lax.psum(grad_down_w.astype(jnp.bfloat16), ("context", "dp")).astype(jnp.float32),
     )
     total_g1, total_q, total_k, total_v, total_o, total_g2, total_r = lax.psum(
-        (
-            grad_gain_one,
-            grad_query_w,
-            grad_key_w,
-            grad_value_w,
-            grad_out_w,
-            grad_gain_two,
-            grad_router_w,
+        lax.psum(
+            (
+                grad_gain_one,
+                grad_query_w,
+                grad_key_w,
+                grad_value_w,
+                grad_out_w,
+                grad_gain_two,
+                grad_router_w,
+            ),
+            axis_name=("context", "dp"),
         ),
-        ("expert", "context", "dp"),
+        axis_name="expert",
     )
     return (
         outputs,

time: 1170 us -> 1580 us (1.35)
  waiting for transfers between devices: 675 us -> 1100 us
  blocking collectives: 187 us -> 171 us
    psum x0 -> x1, waiting for transfers between devices: none -> 209 us  [body(): lax.psum(lax.psum((grad_gain_one, grad_query_w, grad_key_w, grad_value_w,...]
    psum x1, waiting for transfers between devices: 228 us -> 383 us  [body(): lax.psum((grad_gain_one, grad_query_w, grad_key_w, grad_value_w, grad_out...]
    psum x1, waiting for transfers between devices: 328 us -> 369 us  [body(): lax.psum(grad_gate_w.astype(jnp.bfloat16), ('context', 'dp'))]
    psum x1, blocking collectives: 42.8 us -> 20.5 us  [body(): lax.psum((grad_gain_one, grad_query_w, grad_key_w, grad_value_w, grad_out...]
    reduce_scatter x1, waiting for transfers between devices: 1.83 us -> 20.2 us  [body(): lax.psum_scatter(grad_values.reshape(seq_rows, KV * HD), 'context', scatt...]
  transfers between devices with their start and end apart: 6 -> 7, of which waited for: 5 -> 7; matrix products, arithmetic and copies ran while one was open for 6% -> 4% of each run, Pallas kernels for 0% -> 0%
where the time goes in v1:
time: 1580 us; the launch traced here: 1570 us
  waiting for transfers between devices  1100 us (70%)
  blocking collectives  171 us (11%)
  matrix products  114 us (7%)
  local copies, waits for them, and re-layouts  94.6 us (6%)
  other arithmetic  60.3 us (4%)
    psum x1, waiting for transfers between devices, body(): lax.psum((grad_gain_one, grad_query_w, grad_key_w, grad_value_w, grad_out...  383 us
    psum x1, waiting for transfers between devices, body(): lax.psum(grad_gate_w.astype(jnp.bfloat16), ('context', 'dp'))  369 us
    psum x1, waiting for transfers between devices, body(): lax.psum(lax.psum((grad_gain_one, grad_query_w, grad_key_w, grad_value_w,...  209 us
    all_to_all x1, blocking collectives, body(): lax.all_to_all(grad_slots, 'expert', split_axis=0, concat_axis=0, tiled=T...  63.3 us
    all_to_all x1, blocking collectives, body(): lax.all_to_all(sent_rows, 'expert', split_axis=0, concat_axis=0, tiled=True)  62.5 us
    all_to_all x1, waiting for transfers between devices, body(): lax.all_to_all(grad_sent, 'expert', split_axis=0, concat_axis=0, tiled=True)  59.2 us
    all_to_all x1, waiting for transfers between devices, body(): lax.all_to_all(produced, 'expert', split_axis=0, concat_axis=0, tiled=True)  57.9 us
  transfers between devices with their start and end apart: 7, of which 7 were waited for; matrix products, arithmetic and copies ran while one was open for 4% of the time, Pallas kernels for 0%

profile of v1, /device:TPU:0, one launch (start us, length us, event | category | flops | bytes accessed | tf_op | source)
XLA Modules:
  0.0 1569.1 jit_solution(11471794016647284078)
XLA Ops:
  13.0 9.9 all_gather.8
  29.8 8.2 all_gather.9
  38.0 4.1 copy.81
  52.5 4.5 reduce-window.6
  57.9 8.1 scatter_custom_fusion
  67.6 8.8 gather_fusion
  76.4 3.7 select_select_fusion
  80.1 62.5 %all_to_all.20 = bf16[4,4,160,1024]{3,2,1,0:T(8,128)(2,1)S(1)} all-to-all(bf16[4,4,160,1024]{3,2,1,0:T(8,128)(2,1)S(1)} %select_select_fusion), channel_id=1, replica_groups=mesh['expert'=4,'context'=2,'dp'=4] {'expert'}, dimensions={0} | all-to-all | bytes 10485760 | tf_op jit(solution)/shard_map/all_to_all | solution.py:174
  142.6 2.9 fusion.26
  146.6 5.4 fusion.15
  152.3 4.9 convert_bitcast_fusion.1
  157.1 3.3 copy.89
  160.4 5.2 all-to-all-start.1
  167.2 57.9 %all-to-all-done.1 = bf16[4,4,160,1024]{3,2,1,0:T(8,128)(2,1)} async-done(((bf16[4,4,160,1024]{3,2,1,0:T(8,128)(2,1)}), bf16[4,4,160,1024]{3,2,1,0:T(8,128)(2,1)}, u32[]{:S(2)}, u32[]{:S(2)}) %all-to-all-start.1) | async-done | bytes 5242912 | tf_op jit(solution)/shard_map/all_to_all | solution.py:183
  225.1 14.1 gather_fusion.2
  239.2 3.3 fusion.2
  242.9 3.4 bitcast_multiply_fusion.1
  246.3 14.8 gather_fusion.1
  261.1 4.0 select_convert_fusion
  265.1 63.3 %all_to_all.21 = bf16[4,4,160,1024]{3,2,1,0:T(8,128)(2,1)} all-to-all(bf16[4,4,160,1024]{3,2,1,0:T(8,128)(2,1)S(1)} %select_convert_fusion), channel_id=1, replica_groups=mesh['expert'=4,'context'=2,'dp'=4] {'expert'}, dimensions={0} | all-to-all | bytes 10485760 | tf_op jit(solution)/shard_map/all_to_all | solution.py:196
  328.4 12.7 fusion.13
  341.2 8.6 fusion.29
  349.8 8.9 fusion.10
  358.8 3.0 copy.92
  361.8 5.1 all-to-all-start.3
  367.1 59.2 %all-to-all-done.3 = bf16[4,4,160,1024]{3,2,1,0:T(8,128)(2,1)} async-done(((bf16[4,4,160,1024]{3,2,1,0:T(8,128)(2,1)}), bf16[4,4,160,1024]{3,2,1,0:T(8,128)(2,1)}, u32[]{:S(2)}, u32[]{:S(2)}) %all-to-all-start.3) | async-done | bytes 5242912 | tf_op jit(solution)/shard_map/all_to_all | solution.py:220
  426.3 14.1 gather_fusion.3
  440.4 8.1 convert_reduce_fusion
  454.8 5.3 fusion.3
  468.6 6.3 fusion.38
  475.2 3.0 convolution_multiply_fusion
  478.5 2.9 fusion.76
  481.3 2.7 fusion.79
  484.1 4.4 reduce-scatter.3.cloned.1.call-done
  491.5 20.2 %reduce-scatter.5.cloned.1.call-done = f32[256,512]{0,1:T(8,128)} async-done(((f32[512,512]{0,1:T(8,128)}), f32[256,512]{0,1:T(8,128)}) %reduce-scatter.5.cloned.1.call-update) | async-done | bytes 524304 | tf_op jit(solution)/shard_map/reduce_scatter | solution.py:280
  511.7 2.9 fusion.82
  514.7 8.9 bitcast_convert_fusion.2
  523.6 8.7 bitcast_convert_fusion.1
  532.4 5.1 bitcast_convert_fusion
  537.8 382.9 %all-reduce.9.cloned.1.call-done = (f32[1024,1024]{1,0:T(8,128)}, f32[1024,512]{1,0:T(8,128)}, f32[1024,512]{1,0:T(8,128)}, f32[1024,1024]{1,0:T(8,128)}, f32[1024,16]{0,1:T(8,128)}) async-done(((f32[1024,1024]{1,0:T(8,128)}, f32[1024,512]{1,0:T(8,128)}, f32[1024,512]{1,0:T(8,128)}, f32[1024,1024]{1,0:T(8,128)}, f32[1024,16]{0,1:T(8,128)}), (f32[1024,1024]{1,0:T(8,128)}, f32[1024,512]{1,0:T(8,128)}, ...) | async-done | bytes 12648464 | tf_op jit(solution)/shard_map/psum | solution.py:314
  926.6 20.5 %all-reduce = (f32[1024]{0:T(1024)S(1)}, f32[1024]{0:T(1024)S(1)}) all-reduce(f32[1024]{0:T(1024)S(1)} %get-tuple-element.15, f32[1024]{0:T(1024)S(1)} %get-tuple-element.13), channel_id=1, replica_groups=mesh['expert'=4,'context'=2,'dp'=4] {'context','dp'}, use_global_device_ids=true, to_apply=%region_24.26 | all-reduce | flops 2048 | bytes 16384 | tf_op jit(solution)/shard_map/psum | solution.py:314
  947.1 6.7 all-reduce.2
  956.5 369.3 %all-reduce.13.cloned.1.call-done = (bf16[4,1024,512]{2,1,0:T(8,128)(2,1)}, bf16[4,1024,512]{2,1,0:T(8,128)(2,1)}, bf16[4,512,1024]{2,1,0:T(8,128)(2,1)}) async-done(((bf16[4,1024,512]{2,1,0:T(8,128)(2,1)}, bf16[4,1024,512]{2,1,0:T(8,128)(2,1)}, bf16[4,512,1024]{2,1,0:T(8,128)(2,1)}), (bf16[4,1024,512]{2,1,0:T(8,128)(2,1)}, bf16[4,1024,512]{2,1,0:T(8,128)(2,1)}, ...) | async-done | bytes 12582928 | tf_op jit(solution)/shard_map/psum | solution.py:309
  1325.8 6.9 convert_element_type.232
  1332.7 4.6 convert_element_type.234
  1337.3 4.4 convert_element_type.236
  1341.8 209.0 %all-reduce.11.cloned.1.call-done = (f32[1024,1024]{1,0:T(8,128)}, f32[1024,512]{1,0:T(8,128)}, f32[1024,512]{1,0:T(8,128)}, f32[1024,1024]{1,0:T(8,128)}, f32[1024,16]{0,1:T(8,128)}) async-done(((f32[1024,1024]{1,0:T(8,128)}, f32[1024,512]{1,0:T(8,128)}, f32[1024,512]{1,0:T(8,128)}, f32[1024,1024]{1,0:T(8,128)}, f32[1024,16]{0,1:T(8,128)}), (f32[1024,1024]{1,0:T(8,128)}, f32[1024,512]{1,0:T(8,128)}, ...) | async-done | bytes 12648464 | tf_op jit(solution)/shard_map/psum | solution.py:313
  1550.8 4.9 copy.147
  (198 shorter events, 62.4 us)
Async XLA Ops:
  7.2 43.3 %copy-start = (bf16[1024,1024]{1,0:T(8,128)(2,1)S(1)}, bf16[1024,1024]{1,0:T(8,128)(2,1)}, u32[]{:S(2)}) copy-start(bf16[1024,1024]{1,0:T(8,128)(2,1)} %param.23) | copy-start | bytes 6291460
  7.2 20.5 %copy-start.3 = (bf16[1,256,1024]{2,1,0:T(8,128)(2,1)S(1)}, bf16[1,256,1024]{2,1,0:T(8,128)(2,1)}, u32[]{:S(2)}) copy-start(bf16[1,256,1024]{2,1,0:T(8,128)(2,1)} %param.16) | copy-start | bytes 1572868
  9.8 32.3 %copy-start.36 = (f32[1024]{0:T(1024)}, f32[1024]{0:T(1024)S(1)}, u32[]{:S(2)}) copy-start(f32[1024]{0:T(1024)S(1)} %convert_element_type.188) | copy-start | bytes 12292
  11.1 31.0 %copy-start.41 = (f32[256]{0:T(256)}, f32[256]{0:T(256)S(1)}, u32[]{:S(2)}) copy-start(f32[256]{0:T(256)S(1)} %add_rsqrt_fusion.1) | copy-start | bytes 3076
  29.7 15.0 copy-start.32
  29.7 15.0 copy-start.34
  38.0 8.3 copy-start.8
  46.3 4.2 copy-start.1
  48.1 4.2 copy-start.43
  50.5 25.9 %copy-start.28 = (bf16[8,64,2,256]{3,1,2,0:T(8,128)(2,1)}, bf16[8,64,2,256]{3,1,2,0:T(8,128)(2,1)S(1)}, u32[]{:S(2)}) copy-start(bf16[8,64,2,256]{3,1,2,0:T(8,128)(2,1)S(1)} %fusion.57) | copy-start | bytes 1572868
  80.1 62.5 %copy-start.15 = (bf16[4,1024,512]{2,1,0:T(8,128)(2,1)S(1)}, bf16[4,1024,512]{2,1,0:T(8,128)(2,1)}, u32[]{:S(2)}) copy-start(bf16[4,1024,512]{2,1,0:T(8,128)(2,1)} %param.26) | copy-start | bytes 12582916
  142.6 4.1 copy-start.14
  146.6 5.6 copy-start.45
  146.6 5.6 copy-start.44
  160.4 5.3 copy-start.38
  160.4 5.5 copy-start.39
  160.4 5.7 copy-start.26
  160.4 64.7 %all-to-all-start.1 = ((bf16[4,4,160,1024]{3,2,1,0:T(8,128)(2,1)}), bf16[4,4,160,1024]{3,2,1,0:T(8,128)(2,1)}, u32[]{:S(2)}, u32[]{:S(2)}) async-start(bf16[4,4,160,1024]{3,2,1,0:T(8,128)(2,1)} %copy.89), calls=%async_computation.1 | async-start | bytes 10485760 | tf_op jit(solution)/shard_map/all_to_all | solution.py:183
  341.2 8.6 copy-start.16
  361.8 64.5 %all-to-all-start.3 = ((bf16[4,4,160,1024]{3,2,1,0:T(8,128)(2,1)}), bf16[4,4,160,1024]{3,2,1,0:T(8,128)(2,1)}, u32[]{:S(2)}, u32[]{:S(2)}) async-start(bf16[4,4,160,1024]{3,2,1,0:T(8,128)(2,1)} %copy.92), calls=%async_computation.3 | async-start | bytes 10485760 | tf_op jit(solution)/shard_map/all_to_all | solution.py:220
  366.8 121.6 %reduce-scatter.3.cloned.1.call-start = ((), (), s32[]{:S(2)}) async-start(), calls=%async_computation.6 | async-start | bytes 1572864 | tf_op jit(solution)/shard_map/reduce_scatter | solution.py:277
  440.4 8.1 copy-start.7
  440.4 8.6 copy-start.27
  449.0 5.8 copy-start.23
  454.8 5.3 slice-start
  454.8 6.1 slice-start.1
  460.9 4.5 copy-start.19
  460.9 4.5 copy-start.21
  467.7 44.0 %reduce-scatter.5.cloned.1.call-start = ((), (), s32[]{:S(2)}) async-start(), calls=%async_computation.7 | async-start | bytes 1572864 | tf_op jit(solution)/shard_map/reduce_scatter | solution.py:280
  468.6 6.6 copy-start.9
  474.9 3.3 copy-start.33
  474.9 3.5 copy-start.4
  474.9 3.5 copy-start.37
  474.9 3.5 copy-start.42
  474.9 445.8 %all-reduce.9.cloned.1.call-start = ((), (), s32[]{:S(2)}) async-start(), calls=%async_computation.8 | async-start | bytes 25296896 | tf_op jit(solution)/shard_map/psum | solution.py:314
  514.6 811.2 %all-reduce.13.cloned.1.call-start = ((), (), s32[]{:S(2)}) async-start(), calls=%async_computation.10 | async-start | bytes 25165824 | tf_op jit(solution)/shard_map/psum | solution.py:309
  514.7 8.9 copy-start.17
  514.7 17.7 %slice-start.2 = ((s8[5242880]{0:T(1024)(128)(4,1)}), s8[4194304]{0:T(1024)(128)(4,1)S(1)}, s32[]{:S(2)}) async-start(s8[5242880]{0:T(1024)(128)(4,1)} %bitcast.293), calls=%async_computation.13 | async-start | bytes 8388608
  523.6 8.7 slice-start.3
  523.6 8.7 copy-start.46
  537.5 1013.3 %all-reduce.11.cloned.1.call-start = ((), (), s32[]{:S(2)}) async-start(), calls=%async_computation.9 | async-start | bytes 25296896 | tf_op jit(solution)/shard_map/psum | solution.py:313
  920.7 4.2 copy-start.30
  920.7 4.2 copy-start.31
  1325.8 6.9 copy-start.12
  1332.7 4.6 copy-start.11
  1550.8 4.9 copy-start.25
  1550.8 6.3 copy-start.24
  1555.7 3.7 copy-start.13
  (10 other events, 22.5 us)
Sparse Core Ops, SparseCore 0:
  467.8 20.5 reduce-scatter.2
  491.3 20.3 reduce-scatter.4
  518.0 402.7 all-reduce.8
  926.5 399.2 all-reduce.12
  1328.6 222.1 all-reduce.10
